TPU v7x, 32 devices: a whole 2x2x4 slice. The times are simulated.
32 devices in a mesh: seq: 8 (over z, core), fsdp: 4 (over y, x).
Axes of the slice: x: 2, y: 2, z: 4, core: 2. Of those that a mesh axis runs over, the one named last changes fastest.
Arguments:
- tokens: bfloat16 [3072, 2048], P('seq'), may hold values from -6 to 6
- w_query: bfloat16 [2048, 512], P('seq', 'fsdp'), may hold values from -0.125 to 0.125
- w_key: bfloat16 [2048, 512], P('seq', 'fsdp'), may hold values from -0.125 to 0.125
- w_value: bfloat16 [2048, 512], P('seq', 'fsdp'), may hold values from -0.125 to 0.125
- norm_gain: float32 [512], P('fsdp'), may hold values from 0.1 to 1.9
- block_mask: int32 [8, 3, 3], P('seq'), may hold values 0 or 1
- cotangent: bfloat16 [3072, 512], P('seq', 'fsdp'), may hold values from -6 to 6
Outputs:
- attended: bfloat16 [3072, 512], P('seq', 'fsdp')
- grad_tokens: bfloat16 [3072, 2048], P('seq', 'fsdp')
- grad_query: bfloat16 [2048, 512], P('seq', 'fsdp')
- grad_key: bfloat16 [2048, 512], P('seq', 'fsdp')
- grad_value: bfloat16 [2048, 512], P('seq', 'fsdp')
All inputs are finite; a program needn't handle non-finite values. No bound on the sum of `block_mask` on one device may be relied on, other than what follows from the above.
Results may differ from a plain program's by a relative error of at most 0.035.
Values may be sent and summed in bfloat16 or wider, within the bound.
A program may use at most 64 MiB of HBM per device.

v0:
```python
import math

import jax
import jax.numpy as jnp
from jax import lax
from jax.sharding import PartitionSpec as P

HDIM = 128
BLOCK = 128
SEG = 384
NB = 3


EPSILON = 1e-06


def entering(array, axis, join, neutral, backward):
    count = lax.axis_size(axis)
    place = lax.axis_index(axis)
    ahead = count - 1 - place if backward else place
    gathered = lax.all_gather(array.astype(jnp.bfloat16), axis)
    state = jnp.zeros_like(array) + jnp.asarray(neutral, array.dtype)

    def one(lap, state):
        source = count - 1 - lap if backward else lap
        return join(state, lax.dynamic_index_in_dim(gathered, source, 0, False).astype(array.dtype))

    return lax.fori_loop(0, ahead, one, state)


def allowed_pairs(pattern):
    positions = jnp.arange(SEG)
    block_ids = positions // BLOCK
    selector = (block_ids[:, None] == jnp.arange(NB)[None, :]).astype(jnp.float32)
    spread_out = jnp.dot(
        jnp.dot(selector, pattern.astype(jnp.float32), precision=lax.Precision.HIGHEST),
        selector.T,
        precision=lax.Precision.HIGHEST,
    )
    same_block = (block_ids[:, None] == block_ids[None, :]) & (
        positions[None, :] <= positions[:, None]
    )
    earlier_block = (block_ids[None, :] < block_ids[:, None]) & (spread_out > 0.5)
    return same_block | earlier_block


def add_states(first_term, second_term):
    return first_term + second_term


def shards(tokens, w_query, w_key, w_value, norm_gain, block_mask, cotangent):
    columns = w_query.shape[1]
    heads_here = columns // HDIM
    allowed = allowed_pairs(block_mask[0])
    full_query, full_key, full_value = (
        lax.all_gather(w_query, "seq", axis=0, tiled=True),
        lax.all_gather(w_key, "seq", axis=0, tiled=True),
        lax.all_gather(w_value, "seq", axis=0, tiled=True),
    )
    weight_cat = jnp.concatenate([full_query, full_key, full_value], axis=1)
    projected = jnp.dot(tokens, weight_cat, preferred_element_type=jnp.float32)
    projected = projected.astype(jnp.bfloat16)
    queries = projected[:, :columns].reshape(SEG, heads_here, HDIM)
    key_heads = projected[:, columns : 2 * columns].reshape(SEG, heads_here, HDIM)
    value_heads = projected[:, 2 * columns :].reshape(SEG, heads_here, HDIM)
    increment = jnp.einsum(
        "thd,the->hde", key_heads, value_heads, preferred_element_type=jnp.float32
    )
    state = entering(increment, "seq", add_states, jnp.zeros_like(increment), False)
    state_low = state.astype(jnp.bfloat16)
    scores = jnp.einsum("shd,thd->hst", queries, key_heads, preferred_element_type=jnp.float32)
    weights = jnp.where(allowed[None], scores, 0.0).astype(jnp.bfloat16)
    mixed = jnp.einsum("shd,hde->she", queries, state_low, preferred_element_type=jnp.float32)
    mixed = mixed + jnp.einsum(
        "hst,the->she", weights, value_heads, preferred_element_type=jnp.float32
    )
    scale = lax.rsqrt(jnp.mean(mixed * mixed, axis=-1, keepdims=True) + EPSILON)
    normed = mixed * scale
    gain_heads = norm_gain.reshape(heads_here, HDIM)
    attended = (normed * gain_heads).reshape(SEG, columns).astype(jnp.bfloat16)
    given = cotangent.reshape(SEG, heads_here, HDIM).astype(jnp.float32) * gain_heads
    d_mixed = (scale * (given - normed * jnp.mean(given * normed, axis=-1, keepdims=True))).astype(
        jnp.bfloat16
    )
    d_state = jnp.einsum("shd,she->hde", queries, d_mixed, preferred_element_type=jnp.float32)
    later = entering(d_state, "seq", add_states, jnp.zeros_like(d_state), True)
    later_low = later.astype(jnp.bfloat16)
    d_scores = jnp.einsum("she,the->hst", d_mixed, value_heads, preferred_element_type=jnp.float32)
    d_weights = jnp.where(allowed[None], d_scores, 0.0).astype(jnp.bfloat16)
    d_queries = jnp.einsum("she,hde->shd", d_mixed, state_low, preferred_element_type=jnp.float32)
    d_queries = d_queries + jnp.einsum(
        "hst,thd->shd", d_weights, key_heads, preferred_element_type=jnp.float32
    )
    d_keys = jnp.einsum("hst,shd->thd", d_weights, queries, preferred_element_type=jnp.float32)
    d_keys = d_keys + jnp.einsum(
        "the,hde->thd", value_heads, later_low, preferred_element_type=jnp.float32
    )
    d_values = jnp.einsum("hst,she->the", weights, d_mixed, preferred_element_type=jnp.float32)
    d_values = d_values + jnp.einsum(
        "thd,hde->the", key_heads, later_low, preferred_element_type=jnp.float32
    )
    grad_cat = jnp.concatenate(
        [part.reshape(SEG, columns).astype(jnp.bfloat16) for part in (d_queries, d_keys, d_values)],
        axis=1,
    )
    input_rows = lax.psum_scatter(
        lax.dot_general(
            weight_cat, grad_cat, (((1,), (1,)), ((), ())), preferred_element_type=jnp.float32
        ).astype(jnp.bfloat16),
        "fsdp",
        scatter_dimension=0,
        tiled=True,
    ).astype(jnp.float32)
    grad_tokens = input_rows.T.astype(jnp.bfloat16)
    weight_rows = lax.psum_scatter(
        lax.dot_general(
            tokens, grad_cat, (((0,), (0,)), ((), ())), preferred_element_type=jnp.float32
        ).astype(jnp.bfloat16),
        "seq",
        scatter_dimension=0,
        tiled=True,
    ).astype(jnp.float32)
    weight_rows = (weight_rows * (1.0 / math.sqrt(SEG * lax.axis_size("seq")))).astype(jnp.bfloat16)
    return (
        attended,
        grad_tokens,
        weight_rows[:, :columns],
        weight_rows[:, columns : 2 * columns],
        weight_rows[:, 2 * columns :],
    )


def solution(mesh):
    placed = (
        P("seq", None),
        P("seq", "fsdp"),
        P("seq", "fsdp"),
        P("seq", "fsdp"),
        P("fsdp"),
        P("seq", None, None),
        P("seq", "fsdp"),
    )
    return jax.shard_map(
        shards,
        mesh=mesh,
        in_specs=placed,
        out_specs=(
            P("seq", "fsdp"),
            P("seq", "fsdp"),
            P("seq", "fsdp"),
            P("seq", "fsdp"),
            P("seq", "fsdp"),
        ),
        check_vma=False,
    )
```

profile of v0, /device:TPU:0, one launch (start us, length us, event | category | flops | bytes accessed | tf_op | source)
XLA Modules:
  0.0 168.0 jit_solution(6248033320658889828)
XLA Ops:
  7.2 0.0 copy-start
  7.2 0.0 copy-start.7
  7.2 0.0 copy-start.8
  7.2 0.0 copy-start.10
  7.2 0.0 reduce-scatter.5.cloned.1.call-start
  7.3 16.9 %all_gather.21 = bf16[2048,128]{1,0:T(8,128)(2,1)S(1)} all-gather(bf16[256,128]{1,0:T(8,128)(2,1)} %param.12), channel_id=1, replica_groups=mesh['seq'=8,'fsdp'=4] {'seq'}, dimensions={0}, use_global_device_ids=true | all-gather | bytes 589824 | tf_op jit(solution)/shard_map/all_gather | solution.py:56
  24.2 0.1 constant_dynamic-update-slice_fusion.2
  24.3 0.0 copy-done.7
  24.3 14.7 %all_gather.22 = bf16[2048,128]{1,0:T(8,128)(2,1)S(1)} all-gather(bf16[256,128]{1,0:T(8,128)(2,1)S(1)} %copy-done.7), channel_id=1, replica_groups=mesh['seq'=8,'fsdp'=4] {'seq'}, dimensions={0}, use_global_device_ids=true | all-gather | bytes 589824 | tf_op jit(solution)/shard_map/all_gather | solution.py:57
  39.0 0.0 copy-done.8
  39.0 15.1 %all_gather.23 = bf16[2048,128]{1,0:T(8,128)(2,1)S(1)} all-gather(bf16[256,128]{1,0:T(8,128)(2,1)S(1)} %copy-done.8), channel_id=1, replica_groups=mesh['seq'=8,'fsdp'=4] {'seq'}, dimensions={0}, use_global_device_ids=true | all-gather | bytes 589824 | tf_op jit(solution)/shard_map/all_gather | solution.py:58
  54.1 0.0 copy-done.10
  54.1 0.3 fusion.18
  54.4 0.6 fusion.6
  55.0 0.1 constant_dynamic-update-slice_fusion.1
  55.1 0.1 constant_dynamic-update-slice_fusion
  55.3 0.0 copy-done
  55.3 0.0 copy-start.1
  55.3 1.0 fusion.3
  56.3 0.1 copy-done.1
  56.4 0.2 convolution_convert_fusion.4
  56.6 0.0 copy-start.6
  56.6 0.0 copy-start.9
  56.6 0.3 fusion.1
  56.9 0.2 fusion.30
  57.2 14.5 %all-gather = bf16[1024,128]{1,0:T(8,128)(2,1)S(1)} all-gather(bf16[128,128]{1,0:T(8,128)(2,1)S(1)} %convolution_convert_fusion.4), channel_id=2, replica_groups=mesh['seq'=8,'fsdp'=4] {'seq'}, dimensions={0}, use_global_device_ids=true | all-gather | bytes 294912 | tf_op jit(solution)/shard_map/all_gather | solution.py:21
  71.7 0.2 multiply_reduce_fusion
  71.9 0.0 copy-done.6
  72.0 0.1 copy.13
  72.1 0.0 copy-done.9
  72.1 0.1 fusion.14
  72.2 0.1 fusion.20
  72.3 0.3 fusion.2
  72.6 0.2 fusion.34
  72.8 0.2 fusion.24
  73.1 0.2 convolution_convert_fusion.3
  73.3 0.2 fusion.54
  73.5 0.2 fusion.12
  73.6 0.0 copy-start.3
  73.7 14.5 %all-gather.1 = bf16[1024,128]{1,0:T(8,128)(2,1)S(1)} all-gather(bf16[128,128]{1,0:T(8,128)(2,1)S(1)} %convolution_convert_fusion.3), channel_id=3, replica_groups=mesh['seq'=8,'fsdp'=4] {'seq'}, dimensions={0}, use_global_device_ids=true | all-gather | bytes 294912 | tf_op jit(solution)/shard_map/all_gather | solution.py:21
  88.2 0.3 while.23
  88.5 0.2 fusion.11
  88.7 0.0 copy-start.4
  88.7 0.2 fusion.10
  88.9 0.0 copy-done.3
  88.9 0.4 copy-done.4
  89.3 0.0 copy-start.5
  89.3 0.6 copy-done.5
  89.9 2.1 %fusion = bf16[2048,384]{0,1:T(8,128)(2,1)} fusion(bf16[384,2048]{1,0:T(8,128)(2,1)S(1)} %copy-done, bf16[384,128]{0,1:T(8,128)(2,1)S(1)} %fusion.10, bf16[384,128]{0,1:T(8,128)(2,1)S(1)} %fusion.11, bf16[384,128]{0,1:T(8,128)(2,1)S(1)} %fusion.12), kind=kOutput, calls=%fused_computation.4 | convolution fusion | flops 605650944 | bytes 3440640 | tf_op jit(solution)/shard_map/dot_general | solution.py:116
  92.1 0.0 copy-start.2
  92.1 0.0 reduce-scatter.5.cloned.1.call-update
  92.1 0.0 reduce-scatter.3.cloned.1.call-start
  92.2 1.3 copy-done.2
  93.5 3.2 %convolution_convert_fusion.1 = bf16[2048,384]{1,0:T(8,128)(2,1)} fusion(bf16[2048,384]{1,0:T(8,128)(2,1)S(1)} %copy-done.2, bf16[384,128]{0,1:T(8,128)(2,1)} %copy-done.5, bf16[384,128]{0,1:T(8,128)(2,1)} %copy-done.4, bf16[384,128]{0,1:T(8,128)(2,1)} %copy-done.3), kind=kOutput, calls=%fused_computation.3 | convolution fusion | flops 605650944 | bytes 3440640 | tf_op jit(solution)/shard_map/dot_general | solution.py:107
  96.7 0.0 reduce-scatter.3.cloned.1.call-update
  96.8 0.8 copy.15
  97.5 30.0 %reduce-scatter.5.cloned.1.call-done = bf16[256,384]{0,1:T(8,128)(2,1)} async-done(((bf16[2048,384]{0,1:T(8,128)(2,1)}), bf16[256,384]{0,1:T(8,128)(2,1)}) %reduce-scatter.5.cloned.1.call-update) | async-done | bytes 196624 | tf_op jit(solution)/shard_map/reduce_scatter | solution.py:115
  127.5 1.0 multiply_convert_fusion
  128.5 0.7 copy.17
  129.2 0.7 copy.18
  129.9 0.7 copy.19
  130.7 28.6 %reduce-scatter.3.cloned.1.call-done = bf16[512,384]{1,0:T(8,128)(2,1)} async-done(((bf16[2048,384]{1,0:T(8,128)(2,1)}), bf16[512,384]{1,0:T(8,128)(2,1)}) %reduce-scatter.3.cloned.1.call-update) | async-done | bytes 393232 | tf_op jit(solution)/shard_map/reduce_scatter | solution.py:106
  159.3 1.9 %copy.16 = bf16[384,512]{1,0:T(8,128)(2,1)} copy(bf16[384,512]{0,1:T(8,128)(2,1)} %bitcast.98) | data formatting | bytes 786432
  (15 shorter events, 0.1 us)
Async XLA Ops:
  7.2 48.1 %copy-start = (bf16[384,2048]{1,0:T(8,128)(2,1)S(1)}, bf16[384,2048]{1,0:T(8,128)(2,1)}, u32[]{:S(2)}) copy-start(bf16[384,2048]{1,0:T(8,128)(2,1)} %param.11) | copy-start | bytes 4718596
  7.2 17.1 %copy-start.7 = (bf16[256,128]{1,0:T(8,128)(2,1)S(1)}, bf16[256,128]{1,0:T(8,128)(2,1)}, u32[]{:S(2)}) copy-start(bf16[256,128]{1,0:T(8,128)(2,1)} %param.13) | copy-start | bytes 196612
  7.2 31.8 %copy-start.8 = (bf16[256,128]{1,0:T(8,128)(2,1)S(1)}, bf16[256,128]{1,0:T(8,128)(2,1)}, u32[]{:S(2)}) copy-start(bf16[256,128]{1,0:T(8,128)(2,1)} %param.14) | copy-start | bytes 196612
  7.2 46.9 %copy-start.10 = (s32[1,3,3]{2,0,1:T(1,128)S(1)}, s32[1,3,3]{2,0,1:T(1,128)}, u32[]{:S(2)}) copy-start(s32[1,3,3]{2,0,1:T(1,128)} %param.16) | copy-start | bytes 112
  7.2 120.3 %reduce-scatter.5.cloned.1.call-start = ((), (), s32[]{:S(2)}) async-start(), calls=%async_computation.3 | async-start | bytes 1769472 | tf_op jit(solution)/shard_map/reduce_scatter | solution.py:115
  55.3 1.2 copy-start.1
  56.6 15.3 %copy-start.6 = (bf16[384,128]{1,0:T(8,128)(2,1)S(1)}, bf16[384,128]{1,0:T(8,128)(2,1)}, u32[]{:S(2)}) copy-start(bf16[384,128]{1,0:T(8,128)(2,1)} %param.17) | copy-start | bytes 294916
  56.6 15.5 %copy-start.9 = (f32[128]{0:T(128)S(1)}, f32[128]{0:T(128)}, u32[]{:S(2)}) copy-start(f32[128]{0:T(128)} %param.15) | copy-start | bytes 1540
  73.6 15.2 %copy-start.3 = (bf16[384,128]{0,1:T(8,128)(2,1)}, bf16[384,128]{0,1:T(8,128)(2,1)S(1)}, u32[]{:S(2)}) copy-start(bf16[384,128]{0,1:T(8,128)(2,1)S(1)} %fusion.12) | copy-start | bytes 294916
  88.7 0.6 copy-start.4
  89.3 0.6 copy-start.5
  92.1 1.4 copy-start.2
  92.1 67.2 %reduce-scatter.3.cloned.1.call-start = ((), (), s32[]{:S(2)}) async-start(), calls=%async_computation.2 | async-start | bytes 1966080 | tf_op jit(solution)/shard_map/reduce_scatter | solution.py:106
Sparse Core Ops, SparseCore 0:
  92.2 35.2 reduce-scatter.4
  130.5 28.7 reduce-scatter.2
where the time goes:
time: 168 us
  blocking collectives  75.8 us (45%)
  waiting for transfers between devices  58.6 us (35%)
  between operations  14.3 us (9%)
  matrix products  9.83 us (6%)
  local copies, waits for them, and re-layouts  7.88 us (5%)
    reduce_scatter x1, waiting for transfers between devices, shards(): lax.psum_scatter(lax.dot_general(tokens, grad_cat, (((0,), (0,)), ((), ()...  30 us
    all_gather x2, blocking collectives, entering(): gathered = lax.all_gather(array.astype(jnp.bfloat16), axis)  29.1 us
    reduce_scatter x1, waiting for transfers between devices, shards(): lax.psum_scatter(lax.dot_general(weight_cat, grad_cat, (((1,), (1,)), (()...  28.6 us
    all_gather x1, blocking collectives, shards(): lax.all_gather(w_query, 'seq', axis=0, tiled=True)  16.9 us
    all_gather x1, blocking collectives, shards(): lax.all_gather(w_value, 'seq', axis=0, tiled=True)  15.1 us
    all_gather x1, blocking collectives, shards(): lax.all_gather(w_key, 'seq', axis=0, tiled=True)  14.7 us
    unnamed x30, local copies, waits for them, and re-layouts  7.73 us
  transfers between devices with their start and end apart: 2, of which 2 were waited for; matrix products, arithmetic and copies ran while one was open for 4% of the time, Pallas kernels for 0%

commit v1 on v0

v1 whole, which is shorter than its diff:
```python
import functools
import math

import jax
import jax.numpy as jnp
from jax import lax
from jax.experimental import pallas as pl
from jax.experimental.pallas import tpu as pltpu
from jax.sharding import PartitionSpec as P

HDIM = 128
BLOCK = 128
NB = 3
EPSILON = 1e-06
MESH = pl.DeviceIdType.MESH
BF = jnp.bfloat16
F32 = jnp.float32


def mm(a, b):
    return jnp.dot(a, b, preferred_element_type=F32)


def mm_nt(a, b):
    return lax.dot_general(a, b, (((1,), (1,)), ((), ())), preferred_element_type=F32)


def mm_tn(a, b):
    return lax.dot_general(a, b, (((0,), (0,)), ((), ())), preferred_element_type=F32)


def kernel(
    nz, nf,
    tok_hbm, wq_hbm, wk_hbm, wv_hbm, gain_ref, mask_ref, cot_ref,
    att_ref, gt_ref, gq_ref, gk_ref, gv_ref,
    tok, tok_t, wfull, woth, allow,
    inc_out, inc_in, inc_pair, tot_out, tot_in, run,
    dst_out, dst_in, dst_pair, dtot_out, dtot_in, drun,
    gq_own, gkv_own, gq_oth, gkv_oth,
    psq, prq, csq, crq, clq, mineq,
    psk, prk, csk, crk, clk, minek,
    load_sem, w_rs, w_rr, w_ls, w_lr, w_ps, w_pr, wo_s, wo_r, wop_s, wop_r,
    st_s, st_r, stp, tp, ds_s, ds_r, dsp, dtp,
    gq_s, gq_r, gkv_s, gkv_r,
    pq_s, pq_r, cq_s, cq_r, lq_s, lq_r,
    pk_s, pk_r, ck_s, ck_r, lk_s, lk_r,
):
    me = lax.axis_index("seq")
    f = lax.axis_index("fsdp")
    z = me // 2
    k = me - 2 * z
    other = 2 * z + 1 - k
    depth = wq_hbm.shape[0]
    seg = tok.shape[0]

    def rcopy(src, dst, ss, rs, to_seq, to_f):
        return pltpu.make_async_remote_copy(
            src_ref=src, dst_ref=dst, send_sem=ss, recv_sem=rs,
            device_id=(to_seq, to_f), device_id_type=MESH,
        )

    def rows_of(index):
        return pl.ds(pl.multiple_of(index * depth, depth), depth)

    loads = [
        pltpu.make_async_copy(w, wfull.at[rows_of(me), pl.ds(i * HDIM, HDIM)], load_sem.at[i])
        for i, w in enumerate((wq_hbm, wk_hbm, wv_hbm))
    ]
    loads.append(pltpu.make_async_copy(tok_hbm, tok, load_sem.at[3]))
    for c in loads:
        c.start()

    barrier = pltpu.get_barrier_semaphore()
    for t in range(1, nz):
        pl.semaphore_signal(
            barrier, inc=1, device_id=(2 * lax.rem(z + t, nz) + k, f), device_id_type=MESH
        )
    pl.semaphore_signal(barrier, inc=1, device_id=(other, f), device_id_type=MESH)
    for t in range(1, nf):
        pl.semaphore_signal(
            barrier, inc=1, device_id=(me, lax.rem(f + t, nf)), device_id_type=MESH
        )
    for c in loads[:3]:
        c.wait()
    pl.semaphore_wait(barrier, nz - 1 + 1 + nf - 1)

    def w_right(s):
        r = rows_of(2 * (z - s) + k)
        return rcopy(wfull.at[r], wfull.at[r], w_rs.at[s], w_rr.at[s], 2 * (z + 1) + k, f)

    def w_left(s):
        r = rows_of(2 * (z + s) + k)
        return rcopy(wfull.at[r], wfull.at[r], w_ls.at[s], w_lr.at[s], 2 * (z - 1) + k, f)

    def w_pair(j):
        r = rows_of(2 * j + k)
        return rcopy(wfull.at[r], wfull.at[r], w_ps.at[j], w_pr.at[j], other, f)

    half = pl.ds(pl.multiple_of(k * depth, depth), depth)

    def w_across(j):
        return rcopy(
            wfull.at[rows_of(2 * j + k)], woth.at[f, half], wo_s.at[j], wo_r.at[f], me, j
        )

    def w_across_pair(j):
        return rcopy(woth.at[j, half], woth.at[j, half], wop_s.at[j], wop_r.at[j], other, f)

    def spread(j):
        w_pair(j).start()

        @pl.when(j != f)
        def _():
            w_across(j).start()

    def right_has(s):
        return (z < nz - 1) & (z >= s)

    def left_has(s):
        return (z > 0) & (z + s <= nz - 1)

    for s in range(nz - 1):
        @pl.when(right_has(s))
        def _():
            w_right(s).start()

        @pl.when(left_has(s))
        def _():
            w_left(s).start()

        if s == 0:
            spread(z)
            loads[3].wait()
            tok_t[...] = tok[...].T
            row = lax.broadcasted_iota(jnp.int32, (seg, seg), 0)
            col = lax.broadcasted_iota(jnp.int32, (seg, seg), 1)
            zero = jnp.zeros((seg, seg), F32)
            total = jnp.where(col <= row, 1.0, zero)
            for a in range(NB):
                for b in range(a):
                    inside = (
                        (row >= a * BLOCK) & (row < (a + 1) * BLOCK)
                        & (col >= b * BLOCK) & (col < (b + 1) * BLOCK)
                    )
                    m = (mask_ref[0, a, b] == 1).astype(F32)
                    total = jnp.where(inside, zero + m, total)
            allow[...] = total

        @pl.when(z - 1 - s >= 0)
        def _():
            r = rows_of(2 * (z - 1 - s) + k)
            rcopy(wfull.at[r], wfull.at[r], w_rs.at[s], w_rr.at[s], other, f).wait_recv()
            spread(z - 1 - s)

        @pl.when(z + 1 + s <= nz - 1)
        def _():
            r = rows_of(2 * (z + 1 + s) + k)
            rcopy(wfull.at[r], wfull.at[r], w_ls.at[s], w_lr.at[s], other, f).wait_recv()
            spread(z + 1 + s)

    for j in range(nz):
        r = rows_of(2 * j + 1 - k)
        rcopy(wfull.at[r], wfull.at[r], w_ps.at[j], w_pr.at[j], other, f).wait_recv()

    projected = mm(tok[...], wfull[...]).astype(BF)
    q = projected[:, :HDIM]
    key = projected[:, HDIM : 2 * HDIM]
    v = projected[:, 2 * HDIM :]

    def exchange_start(mine, out, inbox, pair_in, s_sem, r_sem, p_sem, backward):
        out[...] = mine.astype(BF)
        for t in range(1, nz):
            there = z - t if backward else z + t

            @pl.when((there >= 0) & (there < nz))
            def _():
                rcopy(
                    out, inbox.at[z], s_sem.at[t], r_sem.at[z], 2 * there + k, f
                ).start()

        @pl.when(k == (1 if backward else 0))
        def _():
            rcopy(out, pair_in, p_sem.at[0], p_sem.at[1], other, f).start()

    def exchange_wait(out, inbox, pair_in, t_out, t_in, acc, r_sem, p_sem, t_sem, backward):
        acc[...] = jnp.zeros_like(acc)
        for t in range(1, nz):
            there = z + t if backward else z - t

            @pl.when((there >= 0) & (there < nz))
            def _():
                rcopy(
                    out, inbox.at[there], p_sem.at[0], r_sem.at[there], other, f
                ).wait_recv()
                acc[...] += inbox[there].astype(F32)

        t_out[...] = acc[...].astype(BF)
        total = rcopy(t_out, t_in, t_sem.at[0], t_sem.at[1], other, f)
        total.start()

        @pl.when(k == (0 if backward else 1))
        def _():
            rcopy(out, pair_in, p_sem.at[0], p_sem.at[1], other, f).wait_recv()
            acc[...] += pair_in[...].astype(F32)

        total.wait()
        return (acc[...] + t_in[...].astype(F32)).astype(BF)

    def exchange_end(out, inbox, pair_in, s_sem, r_sem, p_sem, backward):
        for t in range(1, nz):
            there = z - t if backward else z + t

            @pl.when((there >= 0) & (there < nz))
            def _():
                rcopy(
                    out, inbox.at[z], s_sem.at[t], r_sem.at[z], 2 * there + k, f
                ).wait_send()

        @pl.when(k == (1 if backward else 0))
        def _():
            rcopy(out, pair_in, p_sem.at[0], p_sem.at[1], other, f).wait_send()

    exchange_start(mm_tn(key, v), inc_out, inc_in, inc_pair, st_s, st_r, stp, False)
    ok = allow[...]
    weights = (mm_nt(q, key) * ok).astype(BF)
    mixed = mm(weights, v)
    gain = gain_ref[...]
    given = cot_ref[...].astype(F32) * gain

    state = exchange_wait(inc_out, inc_in, inc_pair, tot_out, tot_in, run, st_r, stp, tp, False)
    mixed = mixed + mm(q, state)
    scale = lax.rsqrt(jnp.mean(mixed * mixed, axis=-1, keepdims=True) + EPSILON)
    normed = mixed * scale
    d_mixed = (
        scale * (given - normed * jnp.mean(given * normed, axis=-1, keepdims=True))
    ).astype(BF)
    exchange_start(mm_tn(q, d_mixed), dst_out, dst_in, dst_pair, ds_s, ds_r, dsp, True)
    att_ref[...] = (normed * gain).astype(BF)
    d_weights = (mm_nt(d_mixed, v) * ok).astype(BF)
    gq_own[...] = (mm_nt(d_mixed, state) + mm(d_weights, key)).astype(BF)

    def across(own, oth, s_sem, r_sem, t):
        there = lax.rem(f + t, nf)
        return rcopy(own, oth.at[f], s_sem.at[t], r_sem.at[f], me, there)

    def across_wait(own, oth, s_sem, r_sem, t):
        there = lax.rem(f + t, nf)
        rcopy(own, oth.at[there], s_sem.at[t], r_sem.at[there], other, f).wait_recv()
        return there

    def rs_start(g, ps, pr, p_s, p_r):
        grads = g[...]
        for j in range(nz):
            ps[j] = mm(tok_t[rows_of(2 * j + 1 - k)], grads).astype(BF)
            rcopy(ps.at[j], pr.at[j], p_s.at[j], p_r.at[j], other, f).start()

    def rs_mine(g, mine):
        grads = g[...]
        for j in range(nz):
            mine[j] = mm(tok_t[rows_of(2 * j + k)], grads)

    def rs_chain(ps, pr, cs, cr, cl, mine, p_s, p_r, c_s, c_r, l_s, l_r):
        for j in range(nz):
            rcopy(ps.at[j], pr.at[j], p_s.at[j], p_r.at[j], other, f).wait_recv()
            mine[j] += pr[j].astype(F32)
        for i in range(nz - 1):
            j = nz - 1 - i

            @pl.when(z < j)
            def _():
                @pl.when(z > 0)
                def _():
                    rcopy(cs.at[j], cr.at[j], c_s.at[j], c_r.at[j], other, f).wait_recv()
                    cs[j] = (mine[j] + cr[j].astype(F32)).astype(BF)

                @pl.when(z == 0)
                def _():
                    cs[j] = mine[j].astype(BF)

                rcopy(cs.at[j], cr.at[j], c_s.at[j], c_r.at[j], 2 * (z + 1) + k, f).start()

            @pl.when(z > i)
            def _():
                @pl.when(z < nz - 1)
                def _():
                    rcopy(cs.at[i], cl.at[i], l_s.at[i], l_r.at[i], other, f).wait_recv()
                    cs[i] = (mine[i] + cl[i].astype(F32)).astype(BF)

                @pl.when(z == nz - 1)
                def _():
                    cs[i] = mine[i].astype(BF)

                rcopy(cs.at[i], cl.at[i], l_s.at[i], l_r.at[i], 2 * (z - 1) + k, f).start()

    def rs_end(ps, pr, cs, cr, cl, mine, p_s, p_r, c_s, c_r, l_s, l_r):
        @pl.when(z > 0)
        def _():
            rcopy(cs.at[z], cr.at[z], c_s.at[z], c_r.at[z], other, f).wait_recv()
            mine[z] += cr[z].astype(F32)

        @pl.when(z < nz - 1)
        def _():
            rcopy(cs.at[z], cl.at[z], l_s.at[z], l_r.at[z], other, f).wait_recv()
            mine[z] += cl[z].astype(F32)

        return mine[z] * (1.0 / math.sqrt(seg * 2 * nz))

    def rs_drain(ps, pr, cs, cr, cl, mine, p_s, p_r, c_s, c_r, l_s, l_r):
        for j in range(nz):
            rcopy(ps.at[j], pr.at[j], p_s.at[j], p_r.at[j], other, f).wait_send()

            @pl.when(z < j)
            def _():
                rcopy(cs.at[j], cr.at[j], c_s.at[j], c_r.at[j], other, f).wait_send()

            @pl.when(z > j)
            def _():
                rcopy(cs.at[j], cl.at[j], l_s.at[j], l_r.at[j], other, f).wait_send()

    q_set = (psq, prq, csq, crq, clq, mineq, pq_s, pq_r, cq_s, cq_r, lq_s, lq_r)
    k_set = (psk, prk, csk, crk, clk, minek, pk_s, pk_r, ck_s, ck_r, lk_s, lk_r)

    for t in range(1, nf):
        across(gq_own, gq_oth, gq_s, gq_r, t).start()
    rs_start(gq_own, psq, prq, pq_s, pq_r)
    for t in range(1, nf):
        there = lax.rem(f + t, nf)
        rcopy(
            wfull.at[rows_of(me)], woth.at[there, half], wo_s.at[there], wo_r.at[there], other, f
        ).wait_recv()
        w_across_pair(there).start()
    d_keys = mm_tn(d_weights, q)
    d_values = mm_tn(weights, d_mixed)
    rs_mine(gq_own, mineq)

    later = exchange_wait(dst_out, dst_in, dst_pair, dtot_out, dtot_in, drun, ds_r, dsp, dtp, True)
    gkv_own[:, :HDIM] = (d_keys + mm_nt(v, later)).astype(BF)
    gkv_own[:, HDIM:] = (d_values + mm(key, later)).astype(BF)
    for t in range(1, nf):
        across(gkv_own, gkv_oth, gkv_s, gkv_r, t).start()
    rs_start(gkv_own, psk, prk, pk_s, pk_r)
    rs_chain(*q_set)
    rs_mine(gkv_own, minek)
    rs_chain(*k_set)

    mine_rows = pl.ds(pl.multiple_of(f * 2 * depth, depth), 2 * depth)
    total = mm_nt(gq_own[...], wfull[mine_rows, :HDIM])
    total = total + mm_nt(gkv_own[...], wfull[mine_rows, HDIM:])
    away = pl.ds(pl.multiple_of((1 - k) * depth, depth), depth)
    for t in range(1, nf):
        there = lax.rem(f + t, nf)
        rcopy(
            woth.at[there, away], woth.at[there, away], wop_s.at[there], wop_r.at[there], other, f
        ).wait_recv()
        across_wait(gq_own, gq_oth, gq_s, gq_r, t)
        across_wait(gkv_own, gkv_oth, gkv_s, gkv_r, t)
        total = total + mm_nt(gq_oth[there], woth[there, :, :HDIM])
        total = total + mm_nt(gkv_oth[there], woth[there, :, HDIM:])
    gt_ref[...] = total.astype(BF)

    gq_ref[...] = rs_end(*q_set).astype(BF)
    both = rs_end(*k_set)
    gk_ref[...] = both[:, :HDIM].astype(BF)
    gv_ref[...] = both[:, HDIM:].astype(BF)

    for s in range(nz - 1):
        @pl.when(right_has(s))
        def _():
            w_right(s).wait_send()

        @pl.when(left_has(s))
        def _():
            w_left(s).wait_send()

    for j in range(nz):
        w_pair(j).wait_send()

        @pl.when(f != j)
        def _():
            w_across(j).wait_send()
            w_across_pair(j).wait_send()

    exchange_end(inc_out, inc_in, inc_pair, st_s, st_r, stp, False)
    exchange_end(dst_out, dst_in, dst_pair, ds_s, ds_r, dsp, True)
    for t in range(1, nf):
        across(gq_own, gq_oth, gq_s, gq_r, t).wait_send()
        across(gkv_own, gkv_oth, gkv_s, gkv_r, t).wait_send()
    rs_drain(*q_set)
    rs_drain(*k_set)


def shards(nz, nf, tokens, w_query, w_key, w_value, norm_gain, block_mask, cotangent):
    seg, features = tokens.shape
    depth, columns = w_query.shape
    vm = pl.BlockSpec(memory_space=pltpu.VMEM)
    hbm = pl.BlockSpec(memory_space=pl.ANY)
    dma = pltpu.SemaphoreType.DMA
    wide = 3 * columns

    def buf(*shape, kind=BF):
        return pltpu.VMEM(shape, kind)

    def exchange_bufs():
        return [
            buf(HDIM, HDIM), buf(nz, HDIM, HDIM), buf(HDIM, HDIM),
            buf(HDIM, HDIM), buf(HDIM, HDIM), buf(HDIM, HDIM, kind=F32),
        ]

    def rs_bufs(width):
        return [buf(nz, depth, width) for _ in range(5)] + [buf(nz, depth, width, kind=F32)]

    one = dma((nz,))
    exchange_sems = [dma((nz,)), dma((nz,)), dma((2,)), dma((2,))]
    scratch = (
        [
            buf(seg, features), buf(features, seg), buf(features, wide),
            buf(nf, 2 * depth, wide), buf(seg, seg, kind=F32),
        ]
        + exchange_bufs() + exchange_bufs()
        + [
            buf(seg, HDIM), buf(seg, 2 * HDIM),
            buf(nf, seg, HDIM), buf(nf, seg, 2 * HDIM),
        ]
        + rs_bufs(HDIM) + rs_bufs(2 * HDIM)
        + [dma((4,)), one, one, one, one, one, one, dma((nf,)), dma((nf,)), dma((nf,)), dma((nf,))]
        + exchange_sems + exchange_sems
        + [dma((nf,))] * 4
        + [one] * 12
    )
    return pl.pallas_call(
        functools.partial(kernel, nz, nf),
        out_shape=(
            jax.ShapeDtypeStruct((seg, columns), BF),
            jax.ShapeDtypeStruct((seg, features // nf), BF),
            jax.ShapeDtypeStruct((depth, columns), BF),
            jax.ShapeDtypeStruct((depth, columns), BF),
            jax.ShapeDtypeStruct((depth, columns), BF),
        ),
        in_specs=[hbm, hbm, hbm, hbm, vm, pl.BlockSpec(memory_space=pltpu.SMEM), vm],
        out_specs=(vm,) * 5,
        scratch_shapes=scratch,
        compiler_params=pltpu.CompilerParams(
            collective_id=0, has_side_effects=True, vmem_limit_bytes=40 * 1024 * 1024
        ),
    )(
        tokens, w_query, w_key, w_value, norm_gain.reshape(1, columns), block_mask, cotangent
    )


def solution(mesh):
    nz, nf = mesh.shape["seq"] // 2, mesh.shape["fsdp"]
    assert nz == nf
    placed = (
        P("seq", None),
        P("seq", "fsdp"),
        P("seq", "fsdp"),
        P("seq", "fsdp"),
        P("fsdp"),
        P("seq", None, None),
        P("seq", "fsdp"),
    )
    return jax.shard_map(
        functools.partial(shards, nz, nf),
        mesh=mesh,
        in_specs=placed,
        out_specs=(P("seq", "fsdp"),) * 5,
        check_vma=False,
    )
```

time: 168 us -> 71.9 us (0.43)
  blocking collectives: 75.8 us -> 0 us
  Pallas kernels: 0 us -> 61.5 us
  waiting for transfers between devices: 58.6 us -> 0 us
  between operations: 14.3 us -> 0.65 us
  matrix products: 9.83 us -> 0 us
    all_gather x5 -> x0, blocking collectives: 75.8 us -> none  [the longest x2 29.1 us: entering(): gathered = lax.all_gather(array.astype(jnp.bfloat16), axis)]
    pallas_call x0 -> x1, Pallas kernels: none -> 61.5 us  [shards(): pl.pallas_call(functools.partial(kernel, nz, nf), out_shape=(jax.ShapeDty...]
    reduce_scatter x2 -> x0, waiting for transfers between devices: 58.6 us -> none  [the longest x1 30 us: shards(): lax.psum_scatter(lax.dot_general(tokens, grad_cat, (((0,), (0,)), ((), ()...]
    dot_general x17 -> x0, matrix products: 9.83 us -> none  [the longest x1 3.25 us: shards(): lax.dot_general(weight_cat, grad_cat, (((1,), (1,)), ((), ())), preferred...]
    unnamed x30 -> x18, local copies, waits for them, and re-layouts: 7.73 us -> 9.43 us
  transfers between devices with their start and end apart: 2 -> 0, of which waited for: 2 -> 0; matrix products, arithmetic and copies ran while one was open for 4% -> 0% of each run, Pallas kernels for 0% -> 0%
where the time goes in v1:
time: 71.9 us; the launch traced here: 71.5 us
  Pallas kernels  61.5 us (86%)
  local copies, waits for them, and re-layouts  9.43 us (13%)
    pallas_call x1, Pallas kernels, shards(): pl.pallas_call(functools.partial(kernel, nz, nf), out_shape=(jax.ShapeDty...  61.5 us
    unnamed x18, local copies, waits for them, and re-layouts  9.43 us

profile of v1, /device:TPU:0, one launch (start us, length us, event | category | flops | bytes accessed | tf_op | source)
XLA Modules:
  0.0 71.5 jit_solution(1745613980171820875)
XLA Ops:
  0.6 0.7 copy.12.mask_ref
  1.3 0.0 copy-start
  1.3 1.4 %copy-done = bf16[384,2048]{1,0:T(8,128)(2,1)S(1)} copy-done((bf16[384,2048]{1,0:T(8,128)(2,1)S(1)}, bf16[384,2048]{1,0:T(8,128)(2,1)}, u32[]{:S(2)}) %copy-start) | copy-done | bytes 1572888
  2.7 0.0 copy-start.1
  2.7 0.9 %copy-done.1 = bf16[384,128]{1,0:T(8,128)(2,1)S(1)} copy-done((bf16[384,128]{1,0:T(8,128)(2,1)S(1)}, bf16[384,128]{1,0:T(8,128)(2,1)}, u32[]{:S(2)}) %copy-start.1) | copy-done | bytes 98328
  3.6 0.0 copy-start.2
  3.6 0.8 %copy-done.2 = bf16[256,128]{1,0:T(8,128)(2,1)S(1)} copy-done((bf16[256,128]{1,0:T(8,128)(2,1)S(1)}, bf16[256,128]{1,0:T(8,128)(2,1)}, u32[]{:S(2)}) %copy-start.2) | copy-done | bytes 65560
  4.5 0.0 copy-start.3
  4.5 0.8 %copy-done.3 = bf16[256,128]{1,0:T(8,128)(2,1)S(1)} copy-done((bf16[256,128]{1,0:T(8,128)(2,1)S(1)}, bf16[256,128]{1,0:T(8,128)(2,1)}, u32[]{:S(2)}) %copy-start.3) | copy-done | bytes 65560
  5.3 0.0 copy-start.4
  5.3 0.8 %copy-done.4 = bf16[256,128]{1,0:T(8,128)(2,1)S(1)} copy-done((bf16[256,128]{1,0:T(8,128)(2,1)S(1)}, bf16[256,128]{1,0:T(8,128)(2,1)}, u32[]{:S(2)}) %copy-start.4) | copy-done | bytes 65560
  6.1 0.0 copy-start.5
  6.1 0.7 copy-done.5
  6.8 61.5 %shard_map.110 = (bf16[384,128]{1,0:T(8,128)(2,1)S(1)}, bf16[384,512]{1,0:T(8,128)(2,1)S(1)}, bf16[256,128]{1,0:T(8,128)(2,1)S(1)}, bf16[256,128]{1,0:T(8,128)(2,1)S(1)}, bf16[256,128]{1,0:T(8,128)(2,1)S(1)}) custom-call(bf16[384,2048]{1,0:T(8,128)(2,1)S(1)} %copy-done, bf16[256,128]{1,0:T(8,128)(2,1)S(1)} %copy-done.2, bf16[256,128]{1,0:T(8,128)(2,1)S(1)} %copy-done.3, ...), custom_call_target="tpu_custom_call" | custom-call | tf_op jit(solution)/shard_map/pallas_call | solution.py:430
  68.3 0.6 copy.18
  68.9 0.7 %copy.19 = bf16[384,512]{1,0:T(8,128)(2,1)} copy(bf16[384,512]{1,0:T(8,128)(2,1)S(1)} %get-tuple-element.11) | data formatting | bytes 786432
  69.7 0.6 copy.20
  70.3 0.6 copy.21
  70.9 0.6 copy.22
Async XLA Ops:
  1.3 1.4 %copy-start = (bf16[384,2048]{1,0:T(8,128)(2,1)S(1)}, bf16[384,2048]{1,0:T(8,128)(2,1)}, u32[]{:S(2)}) copy-start(bf16[384,2048]{1,0:T(8,128)(2,1)} %tok_hbm.1) | copy-start | bytes 4718596
  2.7 0.9 %copy-start.1 = (bf16[384,128]{1,0:T(8,128)(2,1)S(1)}, bf16[384,128]{1,0:T(8,128)(2,1)}, u32[]{:S(2)}) copy-start(bf16[384,128]{1,0:T(8,128)(2,1)} %cot_ref.1) | copy-start | bytes 294916
  3.6 0.8 %copy-start.2 = (bf16[256,128]{1,0:T(8,128)(2,1)S(1)}, bf16[256,128]{1,0:T(8,128)(2,1)}, u32[]{:S(2)}) copy-start(bf16[256,128]{1,0:T(8,128)(2,1)} %wq_hbm.1) | copy-start | bytes 196612
  4.5 0.8 %copy-start.3 = (bf16[256,128]{1,0:T(8,128)(2,1)S(1)}, bf16[256,128]{1,0:T(8,128)(2,1)}, u32[]{:S(2)}) copy-start(bf16[256,128]{1,0:T(8,128)(2,1)} %wk_hbm.1) | copy-start | bytes 196612
  5.3 0.8 %copy-start.4 = (bf16[256,128]{1,0:T(8,128)(2,1)S(1)}, bf16[256,128]{1,0:T(8,128)(2,1)}, u32[]{:S(2)}) copy-start(bf16[256,128]{1,0:T(8,128)(2,1)} %wv_hbm.1) | copy-start | bytes 196612
  6.1 0.7 copy-start.5

commit v2 on v1

--- a/solution.py
+++ b/solution.py
@@ -15,6 +15,7 @@
 MESH = pl.DeviceIdType.MESH
 BF = jnp.bfloat16
 F32 = jnp.float32
+LIMIT = 60 * 1024 * 1024
 
 
 def mm(a, b):
@@ -31,9 +32,9 @@
 
 def kernel(
     nz, nf,
-    tok_hbm, wq_hbm, wk_hbm, wv_hbm, gain_ref, mask_ref, cot_ref,
+    tok_hbm, wq_hbm, wk_hbm, wv_hbm, gain_hbm, mask_hbm, cot_hbm,
     att_ref, gt_ref, gq_ref, gk_ref, gv_ref,
-    tok, tok_t, wfull, woth, allow,
+    tok, tok_t, wfull, woth, allow, proj, gain_ref, mask_ref, cot_ref,
     inc_out, inc_in, inc_pair, tot_out, tot_in, run,
     dst_out, dst_in, dst_pair, dtot_out, dtot_in, drun,
     gq_own, gkv_own, gq_oth, gkv_oth,
@@ -67,6 +68,9 @@
         for i, w in enumerate((wq_hbm, wk_hbm, wv_hbm))
     ]
     loads.append(pltpu.make_async_copy(tok_hbm, tok, load_sem.at[3]))
+    loads.append(pltpu.make_async_copy(mask_hbm, mask_ref, load_sem.at[4]))
+    loads.append(pltpu.make_async_copy(gain_hbm, gain_ref, load_sem.at[5]))
+    loads.append(pltpu.make_async_copy(cot_hbm, cot_ref, load_sem.at[6]))
     for c in loads:
         c.start()
 
@@ -84,17 +88,25 @@
         c.wait()
     pl.semaphore_wait(barrier, nz - 1 + 1 + nf - 1)
 
-    def w_right(s):
-        r = rows_of(2 * (z - s) + k)
-        return rcopy(wfull.at[r], wfull.at[r], w_rs.at[s], w_rr.at[s], 2 * (z + 1) + k, f)
-
-    def w_left(s):
-        r = rows_of(2 * (z + s) + k)
-        return rcopy(wfull.at[r], wfull.at[r], w_ls.at[s], w_lr.at[s], 2 * (z - 1) + k, f)
-
-    def w_pair(j):
-        r = rows_of(2 * j + k)
-        return rcopy(wfull.at[r], wfull.at[r], w_ps.at[j], w_pr.at[j], other, f)
+    part = depth // 2
+
+    def part_of(index, u):
+        return pl.ds(pl.multiple_of(index * depth + u * part, part), part)
+
+    def w_right(s, u):
+        r = part_of(2 * (z - s) + k, u)
+        n = 2 * s + u
+        return rcopy(wfull.at[r], wfull.at[r], w_rs.at[n], w_rr.at[n], 2 * (z + 1) + k, f)
+
+    def w_left(s, u):
+        r = part_of(2 * (z + s) + k, u)
+        n = 2 * s + u
+        return rcopy(wfull.at[r], wfull.at[r], w_ls.at[n], w_lr.at[n], 2 * (z - 1) + k, f)
+
+    def w_pair(j, u):
+        r = part_of(2 * j + k, u)
+        n = 2 * j + u
+        return rcopy(wfull.at[r], wfull.at[r], w_ps.at[n], w_pr.at[n], other, f)
 
     half = pl.ds(pl.multiple_of(k * depth, depth), depth)
 
@@ -106,12 +118,18 @@
     def w_across_pair(j):
         return rcopy(woth.at[j, half], woth.at[j, half], wop_s.at[j], wop_r.at[j], other, f)
 
-    def spread(j):
-        w_pair(j).start()
-
+    def send_across(j):
         @pl.when(j != f)
         def _():
             w_across(j).start()
+
+    def add_pair(j):
+        for u in range(2):
+            r = part_of(2 * j + 1 - k, u)
+            n = 2 * j + u
+            rcopy(wfull.at[r], wfull.at[r], w_ps.at[n], w_pr.at[n], other, f).wait_recv()
+        span = pl.ds(pl.multiple_of(j * 2 * depth, 2 * depth), 2 * depth)
+        proj[...] += mm(tok[:, span], wfull[span])
 
     def right_has(s):
         return (z < nz - 1) & (z >= s)
@@ -119,50 +137,86 @@
     def left_has(s):
         return (z > 0) & (z + s <= nz - 1)
 
+    for u in range(2):
+        @pl.when(z < nz - 1)
+        def _():
+            w_right(0, u).start()
+
+        @pl.when(z > 0)
+        def _():
+            w_left(0, u).start()
+
+    for u in range(2):
+        w_pair(z, u).start()
+    send_across(z)
+    for c in loads[3:]:
+        c.wait()
+    tok_t[...] = tok[...].T
+    row = lax.broadcasted_iota(jnp.int32, (seg, seg), 0)
+    col = lax.broadcasted_iota(jnp.int32, (seg, seg), 1)
+    zero = jnp.zeros((seg, seg), F32)
+    total = jnp.where(col <= row, 1.0, zero)
+    for a in range(NB):
+        for b in range(a):
+            inside = (
+                (row >= a * BLOCK) & (row < (a + 1) * BLOCK)
+                & (col >= b * BLOCK) & (col < (b + 1) * BLOCK)
+            )
+            m = jnp.where(mask_ref[a, 0:1, b : b + 1] == 1, 1.0, 0.0)
+            total = jnp.where(inside, m, total)
+    allow[...] = total
+    proj[...] = jnp.zeros_like(proj)
+
     for s in range(nz - 1):
-        @pl.when(right_has(s))
-        def _():
-            w_right(s).start()
-
-        @pl.when(left_has(s))
-        def _():
-            w_left(s).start()
+        for u in range(2):
+            n = 2 * s + u
+
+            @pl.when(z - 1 - s >= 0)
+            def _():
+                r = part_of(2 * (z - 1 - s) + k, u)
+                rcopy(wfull.at[r], wfull.at[r], w_rs.at[n], w_rr.at[n], other, f).wait_recv()
+                if s < nz - 2:
+                    @pl.when(z < nz - 1)
+                    def _():
+                        w_right(s + 1, u).start()
+
+                w_pair(z - 1 - s, u).start()
+                if u == 1:
+                    send_across(z - 1 - s)
+
+            @pl.when(z + 1 + s <= nz - 1)
+            def _():
+                r = part_of(2 * (z + 1 + s) + k, u)
+                rcopy(wfull.at[r], wfull.at[r], w_ls.at[n], w_lr.at[n], other, f).wait_recv()
+                if s < nz - 2:
+                    @pl.when(z > 0)
+                    def _():
+                        w_left(s + 1, u).start()
+
+                w_pair(z + 1 + s, u).start()
+                if u == 1:
+                    send_across(z + 1 + s)
 
         if s == 0:
-            spread(z)
-            loads[3].wait()
-            tok_t[...] = tok[...].T
-            row = lax.broadcasted_iota(jnp.int32, (seg, seg), 0)
-            col = lax.broadcasted_iota(jnp.int32, (seg, seg), 1)
-            zero = jnp.zeros((seg, seg), F32)
-            total = jnp.where(col <= row, 1.0, zero)
-            for a in range(NB):
-                for b in range(a):
-                    inside = (
-                        (row >= a * BLOCK) & (row < (a + 1) * BLOCK)
-                        & (col >= b * BLOCK) & (col < (b + 1) * BLOCK)
-                    )
-                    m = (mask_ref[0, a, b] == 1).astype(F32)
-                    total = jnp.where(inside, zero + m, total)
-            allow[...] = total
-
-        @pl.when(z - 1 - s >= 0)
-        def _():
-            r = rows_of(2 * (z - 1 - s) + k)
-            rcopy(wfull.at[r], wfull.at[r], w_rs.at[s], w_rr.at[s], other, f).wait_recv()
-            spread(z - 1 - s)
-
-        @pl.when(z + 1 + s <= nz - 1)
-        def _():
-            r = rows_of(2 * (z + 1 + s) + k)
-            rcopy(wfull.at[r], wfull.at[r], w_ls.at[s], w_lr.at[s], other, f).wait_recv()
-            spread(z + 1 + s)
-
-    for j in range(nz):
-        r = rows_of(2 * j + 1 - k)
-        rcopy(wfull.at[r], wfull.at[r], w_ps.at[j], w_pr.at[j], other, f).wait_recv()
-
-    projected = mm(tok[...], wfull[...]).astype(BF)
+            add_pair(z)
+        else:
+            @pl.when(z - s >= 0)
+            def _():
+                add_pair(z - s)
+
+            @pl.when(z + s <= nz - 1)
+            def _():
+                add_pair(z + s)
+
+    @pl.when(z == nz - 1)
+    def _():
+        add_pair(0)
+
+    @pl.when(z == 0)
+    def _():
+        add_pair(nz - 1)
+
+    projected = proj[...].astype(BF)
     q = projected[:, :HDIM]
     key = projected[:, HDIM : 2 * HDIM]
     v = projected[:, 2 * HDIM :]
@@ -248,51 +302,62 @@
         rcopy(own, oth.at[there], s_sem.at[t], r_sem.at[there], other, f).wait_recv()
         return there
 
+    order = []
+    for i in range(nz):
+        for j in (nz - 1 - i, i):
+            if j not in order:
+                order.append(j)
+
     def rs_start(g, ps, pr, p_s, p_r):
         grads = g[...]
-        for j in range(nz):
+        for j in order:
             ps[j] = mm(tok_t[rows_of(2 * j + 1 - k)], grads).astype(BF)
             rcopy(ps.at[j], pr.at[j], p_s.at[j], p_r.at[j], other, f).start()
 
     def rs_mine(g, mine):
         grads = g[...]
-        for j in range(nz):
+        for j in order:
             mine[j] = mm(tok_t[rows_of(2 * j + k)], grads)
 
-    def rs_chain(ps, pr, cs, cr, cl, mine, p_s, p_r, c_s, c_r, l_s, l_r):
-        for j in range(nz):
-            rcopy(ps.at[j], pr.at[j], p_s.at[j], p_r.at[j], other, f).wait_recv()
-            mine[j] += pr[j].astype(F32)
+    def rs_ends(ps, pr, cs, cr, cl, mine, p_s, p_r, c_s, c_r, l_s, l_r):
+        @pl.when(z == 0)
+        def _():
+            for j in range(nz - 1, 0, -1):
+                rcopy(ps.at[j], pr.at[j], p_s.at[j], p_r.at[j], other, f).wait_recv()
+                cs[j] = (mine[j] + pr[j].astype(F32)).astype(BF)
+                rcopy(cs.at[j], cr.at[j], c_s.at[j], c_r.at[j], 2 + k, f).start()
+
+        @pl.when(z == nz - 1)
+        def _():
+            for j in range(nz - 1):
+                rcopy(ps.at[j], pr.at[j], p_s.at[j], p_r.at[j], other, f).wait_recv()
+                cs[j] = (mine[j] + pr[j].astype(F32)).astype(BF)
+                rcopy(cs.at[j], cl.at[j], l_s.at[j], l_r.at[j], 2 * (nz - 2) + k, f).start()
+
+    def rs_inner(ps, pr, cs, cr, cl, mine, p_s, p_r, c_s, c_r, l_s, l_r):
         for i in range(nz - 1):
             j = nz - 1 - i
 
-            @pl.when(z < j)
-            def _():
-                @pl.when(z > 0)
-                def _():
-                    rcopy(cs.at[j], cr.at[j], c_s.at[j], c_r.at[j], other, f).wait_recv()
-                    cs[j] = (mine[j] + cr[j].astype(F32)).astype(BF)
-
-                @pl.when(z == 0)
-                def _():
-                    cs[j] = mine[j].astype(BF)
-
+            @pl.when((z < j) & (z > 0))
+            def _():
+                rcopy(ps.at[j], pr.at[j], p_s.at[j], p_r.at[j], other, f).wait_recv()
+                mine[j] += pr[j].astype(F32)
+                rcopy(cs.at[j], cr.at[j], c_s.at[j], c_r.at[j], other, f).wait_recv()
+                cs[j] = (mine[j] + cr[j].astype(F32)).astype(BF)
                 rcopy(cs.at[j], cr.at[j], c_s.at[j], c_r.at[j], 2 * (z + 1) + k, f).start()
 
-            @pl.when(z > i)
-            def _():
-                @pl.when(z < nz - 1)
-                def _():
-                    rcopy(cs.at[i], cl.at[i], l_s.at[i], l_r.at[i], other, f).wait_recv()
-                    cs[i] = (mine[i] + cl[i].astype(F32)).astype(BF)
-
-                @pl.when(z == nz - 1)
-                def _():
-                    cs[i] = mine[i].astype(BF)
-
+            @pl.when((z > i) & (z < nz - 1))
+            def _():
+                rcopy(ps.at[i], pr.at[i], p_s.at[i], p_r.at[i], other, f).wait_recv()
+                mine[i] += pr[i].astype(F32)
+                rcopy(cs.at[i], cl.at[i], l_s.at[i], l_r.at[i], other, f).wait_recv()
+                cs[i] = (mine[i] + cl[i].astype(F32)).astype(BF)
                 rcopy(cs.at[i], cl.at[i], l_s.at[i], l_r.at[i], 2 * (z - 1) + k, f).start()
 
     def rs_end(ps, pr, cs, cr, cl, mine, p_s, p_r, c_s, c_r, l_s, l_r):
+        rcopy(ps.at[z], pr.at[z], p_s.at[z], p_r.at[z], other, f).wait_recv()
+        mine[z] += pr[z].astype(F32)
+
         @pl.when(z > 0)
         def _():
             rcopy(cs.at[z], cr.at[z], c_s.at[z], c_r.at[z], other, f).wait_recv()
@@ -332,6 +397,7 @@
     d_keys = mm_tn(d_weights, q)
     d_values = mm_tn(weights, d_mixed)
     rs_mine(gq_own, mineq)
+    rs_ends(*q_set)
 
     later = exchange_wait(dst_out, dst_in, dst_pair, dtot_out, dtot_in, drun, ds_r, dsp, dtp, True)
     gkv_own[:, :HDIM] = (d_keys + mm_nt(v, later)).astype(BF)
@@ -339,9 +405,10 @@
     for t in range(1, nf):
         across(gkv_own, gkv_oth, gkv_s, gkv_r, t).start()
     rs_start(gkv_own, psk, prk, pk_s, pk_r)
-    rs_chain(*q_set)
     rs_mine(gkv_own, minek)
-    rs_chain(*k_set)
+    rs_inner(*q_set)
+    rs_ends(*k_set)
+    rs_inner(*k_set)
 
     mine_rows = pl.ds(pl.multiple_of(f * 2 * depth, depth), 2 * depth)
     total = mm_nt(gq_own[...], wfull[mine_rows, :HDIM])
@@ -366,14 +433,17 @@
     for s in range(nz - 1):
         @pl.when(right_has(s))
         def _():
-            w_right(s).wait_send()
+            for u in range(2):
+                w_right(s, u).wait_send()
 
         @pl.when(left_has(s))
         def _():
-            w_left(s).wait_send()
+            for u in range(2):
+                w_left(s, u).wait_send()
 
     for j in range(nz):
-        w_pair(j).wait_send()
+        for u in range(2):
+            w_pair(j, u).wait_send()
 
         @pl.when(f != j)
         def _():
@@ -389,6 +459,15 @@
     rs_drain(*k_set)
 
 
+def hand_over(*refs):
+    sems = refs[10]
+    copies = [pltpu.make_async_copy(refs[i], refs[5 + i], sems.at[i]) for i in range(5)]
+    for c in copies:
+        c.start()
+    for c in copies:
+        c.wait()
+
+
 def shards(nz, nf, tokens, w_query, w_key, w_value, norm_gain, block_mask, cotangent):
     seg, features = tokens.shape
     depth, columns = w_query.shape
@@ -415,6 +494,8 @@
         [
             buf(seg, features), buf(features, seg), buf(features, wide),
             buf(nf, 2 * depth, wide), buf(seg, seg, kind=F32),
+            buf(seg, wide, kind=F32), buf(1, columns, kind=F32),
+            buf(NB, 1, NB, kind=jnp.int32), buf(seg, columns),
         ]
         + exchange_bufs() + exchange_bufs()
         + [
@@ -422,12 +503,12 @@
             buf(nf, seg, HDIM), buf(nf, seg, 2 * HDIM),
         ]
         + rs_bufs(HDIM) + rs_bufs(2 * HDIM)
-        + [dma((4,)), one, one, one, one, one, one, dma((nf,)), dma((nf,)), dma((nf,)), dma((nf,))]
+        + [dma((7,))] + [dma((2 * nz,))] * 6 + [ dma((nf,)), dma((nf,)), dma((nf,)), dma((nf,))]
         + exchange_sems + exchange_sems
         + [dma((nf,))] * 4
         + [one] * 12
     )
-    return pl.pallas_call(
+    results = pl.pallas_call(
         functools.partial(kernel, nz, nf),
         out_shape=(
             jax.ShapeDtypeStruct((seg, columns), BF),
@@ -436,15 +517,23 @@
             jax.ShapeDtypeStruct((depth, columns), BF),
             jax.ShapeDtypeStruct((depth, columns), BF),
         ),
-        in_specs=[hbm, hbm, hbm, hbm, vm, pl.BlockSpec(memory_space=pltpu.SMEM), vm],
+        in_specs=[hbm] * 7,
         out_specs=(vm,) * 5,
         scratch_shapes=scratch,
         compiler_params=pltpu.CompilerParams(
-            collective_id=0, has_side_effects=True, vmem_limit_bytes=40 * 1024 * 1024
+            collective_id=0, has_side_effects=True, vmem_limit_bytes=LIMIT
         ),
     )(
-        tokens, w_query, w_key, w_value, norm_gain.reshape(1, columns), block_mask, cotangent
+        tokens, w_query, w_key, w_value, norm_gain.reshape(1, columns),
+        jnp.transpose(block_mask, (1, 0, 2)), cotangent
     )
+    return pl.pallas_call(
+        hand_over,
+        out_shape=tuple(jax.ShapeDtypeStruct(r.shape, r.dtype) for r in results),
+        in_specs=[hbm] * 5,
+        out_specs=(hbm,) * 5,
+        scratch_shapes=[dma((5,))],
+    )(*results)
 
 
 def solution(mesh):

time: 71.9 us -> 79.5 us (1.11)
  Pallas kernels: 61.5 us -> 78.7 us
  local copies, waits for them, and re-layouts: 9.43 us -> 0 us
    pallas_call x0 -> x1, Pallas kernels: none -> 22 us  [shards(): pl.pallas_call(hand_over, out_shape=tuple((jax.ShapeDtypeStruct(r.shape,...]
    unnamed x18 -> x0, local copies, waits for them, and re-layouts: 9.43 us -> none
    pallas_call x1, Pallas kernels: 61.5 us -> 56.7 us  [shards(): pl.pallas_call(functools.partial(kernel, nz, nf), out_shape=(jax.ShapeDty...]
where the time goes in v2:
time: 79.5 us; the launch traced here: 79.4 us
  Pallas kernels  78.7 us (99%)
    pallas_call x1, Pallas kernels, shards(): pl.pallas_call(functools.partial(kernel, nz, nf), out_shape=(jax.ShapeDty...  56.7 us
    pallas_call x1, Pallas kernels, shards(): pl.pallas_call(hand_over, out_shape=tuple((jax.ShapeDtypeStruct(r.shape,...  22 us

profile of v2, /device:TPU:0, one launch (start us, length us, event | category | flops | bytes accessed | tf_op | source)
XLA Modules:
  0.0 79.4 jit_solution(753726641108811114)
XLA Ops:
  0.6 56.7 %shard_map.110 = (bf16[384,128]{1,0:T(8,128)(2,1)}, bf16[384,512]{1,0:T(8,128)(2,1)}, bf16[256,128]{1,0:T(8,128)(2,1)}, bf16[256,128]{1,0:T(8,128)(2,1)}, bf16[256,128]{1,0:T(8,128)(2,1)}) custom-call(bf16[384,2048]{1,0:T(8,128)(2,1)} %tok_hbm.1, bf16[256,128]{1,0:T(8,128)(2,1)} %wq_hbm.1, bf16[256,128]{1,0:T(8,128)(2,1)} %wk_hbm.1, ...), custom_call_target="tpu_custom_call" | custom-call | tf_op jit(solution)/shard_map/pallas_call | solution.py:511
  57.4 22.0 %shard_map.111 = (bf16[384,128]{1,0:T(8,128)(2,1)}, bf16[384,512]{1,0:T(8,128)(2,1)}, bf16[256,128]{1,0:T(8,128)(2,1)}, bf16[256,128]{1,0:T(8,128)(2,1)}, bf16[256,128]{1,0:T(8,128)(2,1)}) custom-call(bf16[384,128]{1,0:T(8,128)(2,1)} %get-tuple-element.10.refs_0_, bf16[384,512]{1,0:T(8,128)(2,1)} %get-tuple-element.11.refs_1_, ...), custom_call_target="tpu_custom_call" | custom-call | tf_op jit(solution)/shard_map/pallas_call | solution.py:530

commit v3 on v2

--- a/solution.py
+++ b/solution.py
@@ -459,15 +459,6 @@
     rs_drain(*k_set)
 
 
-def hand_over(*refs):
-    sems = refs[10]
-    copies = [pltpu.make_async_copy(refs[i], refs[5 + i], sems.at[i]) for i in range(5)]
-    for c in copies:
-        c.start()
-    for c in copies:
-        c.wait()
-
-
 def shards(nz, nf, tokens, w_query, w_key, w_value, norm_gain, block_mask, cotangent):
     seg, features = tokens.shape
     depth, columns = w_query.shape
@@ -508,7 +499,7 @@
         + [dma((nf,))] * 4
         + [one] * 12
     )
-    results = pl.pallas_call(
+    return pl.pallas_call(
         functools.partial(kernel, nz, nf),
         out_shape=(
             jax.ShapeDtypeStruct((seg, columns), BF),
@@ -527,13 +518,6 @@
         tokens, w_query, w_key, w_value, norm_gain.reshape(1, columns),
         jnp.transpose(block_mask, (1, 0, 2)), cotangent
     )
-    return pl.pallas_call(
-        hand_over,
-        out_shape=tuple(jax.ShapeDtypeStruct(r.shape, r.dtype) for r in results),
-        in_specs=[hbm] * 5,
-        out_specs=(hbm,) * 5,
-        scratch_shapes=[dma((5,))],
-    )(*results)
 
 
 def solution(mesh):

time: 79.5 us -> 65.4 us (0.82)
  Pallas kernels: 78.7 us -> 56.7 us
  local copies, waits for them, and re-layouts: 0 us -> 7.72 us
    pallas_call x1 -> x0, Pallas kernels: 22 us -> none  [shards(): pl.pallas_call(hand_over, out_shape=tuple((jax.ShapeDtypeStruct(r.shape,...]
    unnamed x0 -> x5, local copies, waits for them, and re-layouts: none -> 7.72 us
where the time goes in v3:
time: 65.4 us; the launch traced here: 65.1 us
  Pallas kernels  56.7 us (87%)
  local copies, waits for them, and re-layouts  7.72 us (12%)
    pallas_call x1, Pallas kernels, shards(): pl.pallas_call(functools.partial(kernel, nz, nf), out_shape=(jax.ShapeDty...  56.7 us
    unnamed x5, local copies, waits for them, and re-layouts  7.72 us

profile of v3, /device:TPU:0, one launch (start us, length us, event | category | flops | bytes accessed | tf_op | source)
XLA Modules:
  0.0 65.1 jit_solution(5538679670353640386)
XLA Ops:
  0.6 56.7 %shard_map.110 = (bf16[384,128]{1,0:T(8,128)(2,1)}, bf16[384,512]{1,0:T(8,128)(2,1)}, bf16[256,128]{1,0:T(8,128)(2,1)}, bf16[256,128]{1,0:T(8,128)(2,1)}, bf16[256,128]{1,0:T(8,128)(2,1)}) custom-call(bf16[384,2048]{1,0:T(8,128)(2,1)} %tok_hbm.1, bf16[256,128]{1,0:T(8,128)(2,1)} %wq_hbm.1, bf16[256,128]{1,0:T(8,128)(2,1)} %wk_hbm.1, ...), custom_call_target="tpu_custom_call" | custom-call | tf_op jit(solution)/shard_map/pallas_call | solution.py:502
  57.4 1.5 %copy.17 = bf16[384,128]{1,0:T(8,128)(2,1)} copy(bf16[384,128]{1,0:T(8,128)(2,1)} %get-tuple-element.10) | data formatting | bytes 196608
  58.9 1.8 %copy.18 = bf16[384,512]{1,0:T(8,128)(2,1)} copy(bf16[384,512]{1,0:T(8,128)(2,1)} %get-tuple-element.11) | data formatting | bytes 786432
  60.7 1.5 %copy.19 = bf16[256,128]{1,0:T(8,128)(2,1)} copy(bf16[256,128]{1,0:T(8,128)(2,1)} %get-tuple-element.12) | data formatting | bytes 131072
  62.2 1.5 %copy.20 = bf16[256,128]{1,0:T(8,128)(2,1)} copy(bf16[256,128]{1,0:T(8,128)(2,1)} %get-tuple-element.13) | data formatting | bytes 131072
  63.6 1.5 %copy.21 = bf16[256,128]{1,0:T(8,128)(2,1)} copy(bf16[256,128]{1,0:T(8,128)(2,1)} %get-tuple-element.14) | data formatting | bytes 131072
